TPU v7x, 32 devices: a whole 2x2x4 slice. The times are simulated.
32 devices in a mesh: ang: 4 (over y, x), strip: 8 (over z, core).
Axes of the slice: x: 2, y: 2, z: 4, core: 2. Of those that a mesh axis runs over, the one named last changes fastest.
Arguments:
- slab: bfloat16 [4, 2, 1024, 512], P('ang', None, 'strip'), may hold values from -6 to 6
- shear_taps: float32 [4, 4, 4], replicated, may hold values from -1.5 to 1.5
- band_offsets: int32 [4, 4], replicated, may hold values from -64 to 64
- probe: bfloat16 [2, 256, 256], replicated, may hold values from -6 to 6
- scan_rows: int32 [4, 32], P('ang', 'strip'), may hold values from 0 to 127
- scan_columns: int32 [4, 32], P('ang', 'strip'), may hold values from 0 to 256
- frame_counts: int32 [4, 8], P('ang', 'strip'), may hold values from 1 to 4, 16 in all within a row
- amplitudes: bfloat16 [4, 32, 256, 256], P('ang', 'strip'), may hold values from 0.19921875 to 4
Outputs:
- slab_grad: float32 [4, 2, 1024, 512], P('ang', None, 'strip')
Inputs may be any that keep to these rules, and one draw needn't show every extreme that they name: `frame_counts`: for every angle the counts over the 8 strips sum to 16, and some strip has exactly 4 frames.
All inputs are finite; a program needn't handle non-finite values. No bound on the sum of `frame_counts` on one device may be relied on, other than what follows from the above.
Results may differ from a plain program's by a relative error of at most 0.013.
Values may be sent and summed in bfloat16 or wider, within the bound.
A program may use at most 64 MiB of HBM per device.

v0:
```python
import math

import jax
import jax.numpy as jnp
from jax import lax
from jax.sharding import PartitionSpec as P

MAXSHIFT = 64


def with_halo(block, sides, width):
    for axis, dim in sides:
        count = lax.axis_size(axis)
        forward = [(i, i + 1) for i in range(count - 1)]
        backward = [(target, source) for source, target in forward]
        low = lax.ppermute(
            lax.slice_in_dim(block, block.shape[dim] - width, None, axis=dim), axis, forward
        )
        high = lax.ppermute(lax.slice_in_dim(block, 0, width, axis=dim), axis, backward)
        block = jnp.concatenate([low, block, high], axis=dim)
    return block


def shifted(block, axis, distance):
    devices = range(lax.axis_size(axis))
    route = [(i - distance, i) for i in devices if i - distance in devices]
    return lax.ppermute(block, axis, route)


def dft_tables(length):
    index = jnp.arange(length, dtype=jnp.int32)
    product = index[:, None] * index[None, :] % length
    phase = product.astype(jnp.float32) * (2.0 * math.pi / length)
    scale = 1.0 / math.sqrt(length)
    return (
        (jnp.cos(phase) * scale).astype(jnp.bfloat16),
        (jnp.sin(phase) * scale).astype(jnp.bfloat16),
    )


def frame_gradient(patch, probe, amplitudes):
    length = probe.shape[1]
    cosine, sine = dft_tables(length)
    forward_left = jnp.concatenate(
        [jnp.concatenate([cosine, sine], 1), jnp.concatenate([-sine, cosine], 1)], 0
    )
    inverse_left = jnp.concatenate(
        [jnp.concatenate([cosine, -sine], 1), jnp.concatenate([sine, cosine], 1)], 0
    )
    right = jnp.concatenate([cosine, sine], 1)
    probe_real = probe[0].astype(jnp.float32)
    probe_imag = probe[1].astype(jnp.float32)
    patch_real = patch[:, 0]
    patch_imag = patch[:, 1]
    exit_wave = jnp.concatenate(
        [
            probe_real * patch_real - probe_imag * patch_imag,
            probe_real * patch_imag + probe_imag * patch_real,
        ],
        axis=1,
    ).astype(jnp.bfloat16)
    half = jnp.einsum(
        "ij,bjk->bik", forward_left, exit_wave, preferred_element_type=jnp.float32
    ).astype(jnp.bfloat16)
    far = jnp.einsum("bij,jk->bik", half, right, preferred_element_type=jnp.float32)
    far_real = far[:, :length, :length] + far[:, length:, length:]
    far_imag = far[:, length:, :length] - far[:, :length, length:]
    factor = 1.0 - amplitudes.astype(jnp.float32) / jnp.sqrt(
        far_real * far_real + far_imag * far_imag + 1.0
    )
    residual = jnp.concatenate([far_real * factor, far_imag * factor], axis=1).astype(jnp.bfloat16)
    back_half = jnp.einsum(
        "ij,bjk->bik", inverse_left, residual, preferred_element_type=jnp.float32
    ).astype(jnp.bfloat16)
    back = jnp.einsum("bij,jk->bik", back_half, right, preferred_element_type=jnp.float32)
    back_real = back[:, :length, :length] - back[:, length:, length:]
    back_imag = back[:, length:, :length] + back[:, :length, length:]
    grad_real = probe_real * back_real + probe_imag * back_imag
    grad_imag = probe_real * back_imag - probe_imag * back_real
    return jnp.stack([grad_real, grad_imag], axis=1)


def add_taps(total, source, shear_taps, band_offsets, angle, depth, sign, width):
    margin = MAXSHIFT + shear_taps.shape[0]
    for tap in range(shear_taps.shape[0]):
        start = margin + sign * (band_offsets[angle, depth] + tap)
        piece = lax.dynamic_slice_in_dim(source, start, width, axis=2)
        total = total + shear_taps[tap, angle, depth] * piece.astype(jnp.float32)
    return total


def pad_columns(field, margin):
    return jnp.pad(field, ((0, 0), (0, 0), (0, 0), (margin, margin)))


def per_device(
    slab, shear_taps, band_offsets, probe, scan_rows, scan_columns, frame_counts, amplitudes
):
    local_slices = slab.shape[0]
    rows = slab.shape[2]
    width = slab.shape[3]
    local_angles = scan_rows.shape[0]
    slots = scan_rows.shape[1]
    length = probe.shape[1]
    rim_width = length // 2
    margin = MAXSHIFT + shear_taps.shape[0]
    my_index = lax.axis_index("ang")
    angle_base = my_index * local_angles
    piece = lax.all_gather(slab, "ang", axis=0, tiled=True)
    padded = pad_columns(piece, margin)

    def one_angle(which, acc):
        angle = angle_base + which

        def add_slice(inner_index, inner):
            return add_taps(
                inner, padded[inner_index], shear_taps, band_offsets, angle, inner_index, 1, width
            )

        current = lax.fori_loop(0, piece.shape[0], add_slice, acc[which])
        return lax.dynamic_update_index_in_dim(acc, current, which, 0)

    projection = lax.fori_loop(
        0, local_angles, one_angle, jnp.zeros((local_angles, 2, rows, width), jnp.float32)
    )
    extended = with_halo(projection, (("strip", 2),), rim_width)
    count_all = local_angles * slots
    angle_of = jnp.repeat(jnp.arange(local_angles, dtype=jnp.int32), slots)
    row_starts = scan_rows.reshape(count_all)
    column_starts = scan_columns.reshape(count_all)
    anchor = jnp.zeros((), jnp.int32)

    def cut_patch(angle, row, column):
        return lax.dynamic_slice(extended, (angle, anchor, row, column), (1, 2, length, length))[0]

    patches = jax.vmap(cut_patch)(angle_of, row_starts, column_starts)
    live = (
        (jnp.arange(slots, dtype=jnp.int32)[None, :] < frame_counts)
        .astype(jnp.float32)
        .reshape(count_all)
    )
    gradients = (
        frame_gradient(patches, probe, amplitudes.reshape(count_all, length, length))
        * live[:, None, None, None]
    )

    def place(which, acc):
        corner = (angle_of[which], anchor, row_starts[which], column_starts[which])
        current = lax.dynamic_slice(acc, corner, (1, 2, length, length))
        return lax.dynamic_update_slice(acc, current + gradients[which][None], corner)

    placed = lax.fori_loop(0, count_all, place, jnp.zeros(extended.shape, jnp.float32))
    upper = placed[:, :, :rim_width]
    middle = placed[:, :, rim_width : rim_width + rows]
    lower = placed[:, :, rim_width + rows :]
    from_below = shifted(upper.astype(jnp.bfloat16), "strip", -1).astype(upper.dtype)
    from_above = shifted(lower.astype(jnp.bfloat16), "strip", 1).astype(lower.dtype)
    image = middle + from_above
    image = image + from_below
    image = image.astype(jnp.bfloat16)
    slice_base = my_index * local_slices
    fold_piece = lax.all_gather(image, "ang", axis=0, tiled=True)
    fold_padded = pad_columns(fold_piece, margin)

    def one_slice(which, acc):
        depth = slice_base + which

        def add_angle(inner_index, inner):
            return add_taps(
                inner,
                fold_padded[inner_index],
                shear_taps,
                band_offsets,
                inner_index,
                depth,
                -1,
                width,
            )

        current = lax.fori_loop(0, fold_piece.shape[0], add_angle, acc[which])
        return lax.dynamic_update_index_in_dim(acc, current, which, 0)

    return lax.fori_loop(
        0, local_slices, one_slice, jnp.zeros((local_slices, 2, rows, width), jnp.float32)
    )


def solution(mesh):
    return jax.shard_map(
        per_device,
        mesh=mesh,
        in_specs=(
            P("ang", None, "strip", None),
            P(),
            P(),
            P(),
            P("ang", "strip"),
            P("ang", "strip"),
            P("ang", "strip"),
            P("ang", "strip", None, None),
        ),
        out_specs=P("ang", None, "strip", None),
        check_vma=False,
    )
```

profile of v0, /device:TPU:16, one launch (start us, length us, event | category | flops | bytes accessed | tf_op | source)
XLA Modules:
  0.0 249.5 jit_solution(15407708136034549703)
XLA Ops:
  6.5 0.7 all-gather.3.cloned.1.call-update
  7.3 0.7 compare_select_fusion.1
  8.1 0.7 compare_select_fusion
  9.5 1.0 fusion.39
  10.5 1.1 multiply_convert_fusion.2
  11.6 25.3 %all-gather.3.cloned.1.call-done = bf16[4,2,128,512]{3,2,1,0:T(8,128)(2,1)} async-done(((bf16[1,2,128,512]{3,2,1,0:T(8,128)(2,1)}), bf16[4,2,128,512]{3,2,1,0:T(8,128)(2,1)}) %all-gather.3.cloned.1.call-update) | async-done | bytes 1048592 | tf_op jit(solution)/shard_map/all_gather | solution.py:109
  36.9 1.8 pad.7
  38.8 35.3 %while.68 = (s32[]{:T(128)}, f32[2,128,512]{2,1,0:T(8,128)S(1)}, f32[4,4,4]{2,1,0:T(4,128)S(1)}, s32[]{:T(128)}, s32[4,4]{1,0:T(4,128)S(1)}, /*index=5*/bf16[4,2...) while((s32[]{:T(128)}, f32[2,128,512]{2,1,0:T(8,128)S(1)}, ...), condition=%wide.region_1.0_spmd.clone, body=%wide.region_0.1_spmd.clone.sunk | while | flops 1703960 | bytes 2097679 | solution.py:120
  43.9 0.7 constant_dynamic-slice_fusion.13
  44.5 3.1 %bitcast_add_fusion.13 = f32[2,128,512]{2,1,0:T(8,128)S(1)} fusion(f32[2,128,512]{2,1,0:T(8,128)S(1)} %get-tuple-element.896, bf16[4,2,128,648]{3,2,1,0:T(8,128)(2,1)S(1)} %get-tuple-element.918, s32[]{:T(128)S(6)} %select_n.317, s32[]{:T(128)S(6)} %select_n.319, f32[]{:T(128)} %bitcast.168, s32[]{:T(128)S(6)} %select_n.321, f32[]{:T(128)} %bitcast.171, ...), kind=kLoop, calls=%fused_computation.3.clone.1 | loop fusion | flops 1703936 | bytes 2097189 | tf_op jit(solution)/shard_map/while/body/eval_jaxpr/while/body/eval_jaxpr/add | solution.py:88
  52.7 0.7 constant_dynamic-slice_fusion.13
  53.4 3.1 %bitcast_add_fusion.13 = f32[2,128,512]{2,1,0:T(8,128)S(1)} fusion(f32[2,128,512]{2,1,0:T(8,128)S(1)} %get-tuple-element.896, bf16[4,2,128,648]{3,2,1,0:T(8,128)(2,1)S(1)} %get-tuple-element.918, s32[]{:T(128)S(6)} %select_n.317, s32[]{:T(128)S(6)} %select_n.319, f32[]{:T(128)} %bitcast.168, s32[]{:T(128)S(6)} %select_n.321, f32[]{:T(128)} %bitcast.171, ...), kind=kLoop, calls=%fused_computation.3.clone.1 | loop fusion | flops 1703936 | bytes 2097189 | tf_op jit(solution)/shard_map/while/body/eval_jaxpr/while/body/eval_jaxpr/add | solution.py:88
  56.5 0.6 dynamic_slice.270
  61.5 0.7 constant_dynamic-slice_fusion.13
  62.2 3.1 %bitcast_add_fusion.13 = f32[2,128,512]{2,1,0:T(8,128)S(1)} fusion(f32[2,128,512]{2,1,0:T(8,128)S(1)} %get-tuple-element.896, bf16[4,2,128,648]{3,2,1,0:T(8,128)(2,1)S(1)} %get-tuple-element.918, s32[]{:T(128)S(6)} %select_n.317, s32[]{:T(128)S(6)} %select_n.319, f32[]{:T(128)} %bitcast.168, s32[]{:T(128)S(6)} %select_n.321, f32[]{:T(128)} %bitcast.171, ...), kind=kLoop, calls=%fused_computation.3.clone.1 | loop fusion | flops 1703936 | bytes 2097189 | tf_op jit(solution)/shard_map/while/body/eval_jaxpr/while/body/eval_jaxpr/add | solution.py:88
  65.3 0.6 dynamic_slice.270
  70.4 0.7 constant_dynamic-slice_fusion.13
  71.1 3.1 %bitcast_add_fusion.13 = f32[2,128,512]{2,1,0:T(8,128)S(1)} fusion(f32[2,128,512]{2,1,0:T(8,128)S(1)} %get-tuple-element.896, bf16[4,2,128,648]{3,2,1,0:T(8,128)(2,1)S(1)} %get-tuple-element.918, s32[]{:T(128)S(6)} %select_n.317, s32[]{:T(128)S(6)} %select_n.319, f32[]{:T(128)} %bitcast.168, s32[]{:T(128)S(6)} %select_n.321, f32[]{:T(128)} %bitcast.171, ...), kind=kLoop, calls=%fused_computation.3.clone.1 | loop fusion | flops 1703936 | bytes 2097189 | tf_op jit(solution)/shard_map/while/body/eval_jaxpr/while/body/eval_jaxpr/add | solution.py:88
  74.1 1.9 collective-permute-start
  76.1 3.6 %collective-permute-start.1 = (f32[1,2,128,512]{3,2,1,0:T(8,128)S(1)}, f32[1,2,128,512]{3,2,1,0:T(8,128)S(1)}, u32[]{:S(2)}, u32[]{:S(2)}) collective-permute-start(f32[1,2,128,512]{3,2,1,0:T(8,128)S(1)} %bitcast.196), channel_id=1, source_target_pairs={{1,0},{2,1},{3,2},{4,3},{5,4},{6,5},{7,6},{9,8},{10,9},{11,10},{12... | collective-permute-start | bytes 1572872 | tf_op jit(solution)/shard_map/ppermute | solution.py:19
  79.8 4.8 %collective-permute-done = f32[1,2,128,512]{3,2,1,0:T(8,128)S(1)} collective-permute-done((f32[1,2,128,512]{3,2,1,0:T(8,128)S(1)}, f32[1,2,128,512]{3,2,1,0:T(8,128)S(1)}, u32[]{:S(2)}, u32[]{:S(2)}) %collective-permute-start) | collective-permute-done | bytes 524320 | tf_op jit(solution)/shard_map/ppermute | solution.py:16
  84.6 1.8 collective-permute-done.1
  86.5 12.1 %while.67 = (s32[]{:T(128)}, f32[1,2,384,512]{3,2,1,0:T(8,128)S(1)}, s32[4,4]{1,0:T(4,128)S(1)}, f32[4,1,2,256,256]{4,3,0,2,1:T(8,128)}, s32[]{:T(128)}) while((s32[]{:T(128)}, f32[1,2,384,512]{3,2,1,0:T(8,128)S(1)}, s32[4,4]{1,0:T(4,128)S(1)}, f32[4,1,2,256,256]{4,3,0,2,1:T(8,128)}, s32[]{:T(128)}) %tuple.153), condition=%wide.while_cond, body=%wide.while_body.sunk | while | flops 2 | bytes 1050225 | solution.py:134
  86.6 0.7 fusion.47
  87.2 2.3 bitcast_dynamic-update-slice_fusion.2
  89.6 0.7 fusion.47
  90.2 2.4 bitcast_dynamic-update-slice_fusion.2
  92.6 0.7 fusion.47
  93.3 2.3 bitcast_dynamic-update-slice_fusion.2
  95.6 0.7 fusion.47
  96.3 2.4 bitcast_dynamic-update-slice_fusion.2
  98.6 1.8 subtract_convert_fusion
  100.5 3.2 %fusion.1 = f32[4,512,512]{2,1,0:T(8,128)} fusion(bf16[4,256,256]{2,1,0:T(8,128)(2,1)S(1)} %get-tuple-element.720, bf16[4,256,256]{2,1,0:T(8,128)(2,1)S(1)} %get-tuple-element.719, bf16[256,256]{1,0:T(8,128)(2,1)S(1)} %get-tuple-element.726, bf16[256,256]{1,0:T(8,128)(2,1)S(1)} %fusion.39, bf16[256,256]{1,0:T(8,128)(2,1)S(1)} %get-tuple-element.725), kind=kOutput, calls=%fused_computation.24 | convolution fusion | flops 1078984704 | bytes 5636096 | tf_op jit(solution)/shard_map/bij,jk->bik/dot_general | solution.py:65
  103.7 2.7 %multiply_convert_fusion.1 = (bf16[4,256,256]{2,1,0:T(8,128)(2,1)S(1)}, bf16[4,256,256]{2,1,0:T(8,128)(2,1)S(1)}) fusion(bf16[1,4,256,256]{3,2,1,0:T(8,128)(2,1)S(1)} %copy-done.1, f32[4,512,512]{2,1,0:T(8,128)} %fusion.1), kind=kLoop, calls=%fused_computation.44 | loop fusion | flops 3407872 | bytes 5767168 | tf_op jit(solution)/shard_map/convert.5
  106.4 3.2 %fusion.3 = f32[4,512,512]{2,1,0:T(8,128)} fusion(bf16[4,256,256]{2,1,0:T(8,128)(2,1)S(1)} %get-tuple-element.718, bf16[4,256,256]{2,1,0:T(8,128)(2,1)S(1)} %get-tuple-element.717, bf16[256,256]{1,0:T(8,128)(2,1)S(1)} %get-tuple-element.726, bf16[256,256]{1,0:T(8,128)(2,1)S(1)} %get-tuple-element.725, bf16[256,256]{1,0:T(8,128)(2,1)S(1)} %fusion.39), kind=kOutput, calls=%fused_computation.26 | convolution fusion | flops 1078984704 | bytes 5636096 | tf_op jit(solution)/shard_map/bij,jk->bik/dot_general | solution.py:75
  109.6 2.5 %add_bitcast_fusion = (f32[4,1,256,256]{3,2,0,1:T(8,128)S(1)}, f32[4,1,256,256]{3,2,0,1:T(8,128)S(1)}) fusion(f32[256,256]{1,0:T(8,128)S(1)} %get-tuple-element.724, f32[256,256]{1,0:T(8,128)S(1)} %get-tuple-element.723, f32[4,512,512]{2,1,0:T(8,128)} %fusion.3), kind=kLoop, calls=%fused_computation.42 | loop fusion | flops 2097152 | bytes 6815744 | tf_op jit(solution)/shard_map/stack | solution.py:80
  112.1 1.6 maximum_multiply_fusion
  113.9 55.7 %while.66 = (s32[]{:T(128)}, f32[1,2,384,512]{3,2,1,0:T(8,128)S(1)}, s32[4]{0:T(128)S(1)}, s32[4]{0:T(128)S(1)}, f32[4,2,256,256]{3,2,0,1:T(8,128)}, /*index=5*/s32[]{:T(128)}, s32[]{:T(128)}, s32[]{:T(128)}, s32[]{:T(128)}) while((s32[]{:T(128)}, f32[1,2,384,512]{3,2,1,0:T(8,128)S(1)}, s32[4]{0:T(128)S(1)}, s32[4]{0:T(128)S(1)}, ...), condition=%wide.region_3.4_spmd, body=%wide.region_2.0_spmd.sunk | while | flops 131080 | bytes 2621641 | solution.py:152
  119.0 1.3 bitcast_add_fusion.12
  120.3 7.6 %dynamic_update_slice.13 = f32[1,2,384,512]{3,2,1,0:T(8,128)S(1)} dynamic-update-slice(f32[1,2,384,512]{3,2,1,0:T(8,128)S(1)} %get-tuple-element.956, f32[1,2,256,256]{3,2,1,0:T(8,128)S(1)} %bitcast_add_fusion.12, s32[]{:T(128)} %constant.769.clone.1..sunk, s32[]{:T(128)} %constant.769.clone.1..sunk, s32[]{:T(128)S(6)} %select_n.315, s32[]{:T(128)S(6)} %select_n.316) | dynamic-update-slice | bytes 1048580 | tf_op jit(solution)/shard_map/while/body/eval_jaxpr/dynamic_update_slice | solution.py:150
  133.0 1.3 bitcast_add_fusion.12
  134.2 8.0 %dynamic_update_slice.13 = f32[1,2,384,512]{3,2,1,0:T(8,128)S(1)} dynamic-update-slice(f32[1,2,384,512]{3,2,1,0:T(8,128)S(1)} %get-tuple-element.956, f32[1,2,256,256]{3,2,1,0:T(8,128)S(1)} %bitcast_add_fusion.12, s32[]{:T(128)} %constant.769.clone.1..sunk, s32[]{:T(128)} %constant.769.clone.1..sunk, s32[]{:T(128)S(6)} %select_n.315, s32[]{:T(128)S(6)} %select_n.316) | dynamic-update-slice | bytes 1048580 | tf_op jit(solution)/shard_map/while/body/eval_jaxpr/dynamic_update_slice | solution.py:150
  147.3 1.3 bitcast_add_fusion.12
  148.6 7.4 %dynamic_update_slice.13 = f32[1,2,384,512]{3,2,1,0:T(8,128)S(1)} dynamic-update-slice(f32[1,2,384,512]{3,2,1,0:T(8,128)S(1)} %get-tuple-element.956, f32[1,2,256,256]{3,2,1,0:T(8,128)S(1)} %bitcast_add_fusion.12, s32[]{:T(128)} %constant.769.clone.1..sunk, s32[]{:T(128)} %constant.769.clone.1..sunk, s32[]{:T(128)S(6)} %select_n.315, s32[]{:T(128)S(6)} %select_n.316) | dynamic-update-slice | bytes 1048580 | tf_op jit(solution)/shard_map/while/body/eval_jaxpr/dynamic_update_slice | solution.py:150
  161.0 1.3 bitcast_add_fusion.12
  162.3 7.3 %dynamic_update_slice.13 = f32[1,2,384,512]{3,2,1,0:T(8,128)S(1)} dynamic-update-slice(f32[1,2,384,512]{3,2,1,0:T(8,128)S(1)} %get-tuple-element.956, f32[1,2,256,256]{3,2,1,0:T(8,128)S(1)} %bitcast_add_fusion.12, s32[]{:T(128)} %constant.769.clone.1..sunk, s32[]{:T(128)} %constant.769.clone.1..sunk, s32[]{:T(128)S(6)} %select_n.315, s32[]{:T(128)S(6)} %select_n.316) | dynamic-update-slice | bytes 1048580 | tf_op jit(solution)/shard_map/while/body/eval_jaxpr/dynamic_update_slice | solution.py:150
  169.8 5.6 %collective-permute-start.2 = (bf16[1,2,128,512]{3,2,1,0:T(8,128)(2,1)S(1)}, bf16[1,2,128,512]{3,2,1,0:T(8,128)(2,1)S(1)}, u32[]{:S(2)}, u32[]{:S(2)}) collective-permute-start(bf16[1,2,128,512]{3,2,1,0:T(8,128)(2,1)S(1)} %get-tuple-element.721), channel_id=1, source_target_pairs={{0,1},{1,2},{2,3},{3,4},{4,5},{5,6},{6,7},{8,9},{9,10},{10,11},{11... | collective-permute-start | bytes 786440 | tf_op jit(solution)/shard_map/ppermute | solution.py:27
  175.4 1.9 collective-permute-start.3
  177.5 4.2 %collective-permute-done.3 = bf16[1,2,128,512]{3,2,1,0:T(8,128)(2,1)S(1)} collective-permute-done((bf16[1,2,128,512]{3,2,1,0:T(8,128)(2,1)S(1)}, bf16[1,2,128,512]{3,2,1,0:T(8,128)(2,1)S(1)}, u32[]{:S(2)}, u32[]{:S(2)}) %collective-permute-start.3) | collective-permute-done | bytes 262176 | tf_op jit(solution)/shard_map/ppermute | solution.py:27
  181.6 0.8 add_convert_fusion.1
  182.5 29.4 %all-gather.5.cloned.1.call-done = bf16[4,2,128,512]{3,2,1,0:T(8,128)(2,1)} async-done(((bf16[1,2,128,512]{3,2,1,0:T(8,128)(2,1)}), bf16[4,2,128,512]{3,2,1,0:T(8,128)(2,1)}) %all-gather.5.cloned.1.call-update) | async-done | bytes 1048592 | tf_op jit(solution)/shard_map/all_gather | solution.py:162
  211.8 1.8 pad.8
  213.6 28.2 %while.69 = (s32[]{:T(128)}, f32[2,128,512]{2,1,0:T(8,128)S(1)}, f32[4,4,4]{2,1,0:T(4,128)S(1)}, s32[]{:T(128)}, s32[4,4]{1,0:T(4,128)S(1)}, /*index=5*/bf16[4,2...) while((s32[]{:T(128)}, f32[2,128,512]{2,1,0:T(8,128)S(1)}, ...), condition=%wide.region_5.6_spmd.clone, body=%wide.region_4.5_spmd.clone.sunk | while | flops 1703967 | bytes 2097747 | solution.py:180
  216.8 0.7 constant_dynamic-slice_fusion.14
  217.5 3.1 %bitcast_add_fusion.14 = f32[2,128,512]{2,1,0:T(8,128)S(1)} fusion(f32[2,128,512]{2,1,0:T(8,128)S(1)} %get-tuple-element.990, bf16[4,2,128,648]{3,2,1,0:T(8,128)(2,1)S(1)} %get-tuple-element.1010, s32[]{:T(128)S(6)} %select_n.326, s32[]{:T(128)S(6)} %select_n.328, f32[]{:T(128)} %bitcast.184, s32[]{:T(128)S(6)} %select_n.330, f32[]{:T(128)} %bitcast.187, ...), kind=kLoop, calls=%fused_computation.11.clone.1 | loop fusion | flops 1703936 | bytes 2097189 | tf_op jit(solution)/shard_map/while/body/eval_jaxpr/while/body/eval_jaxpr/add | solution.py:88
  223.9 0.7 constant_dynamic-slice_fusion.14
  224.6 3.1 %bitcast_add_fusion.14 = f32[2,128,512]{2,1,0:T(8,128)S(1)} fusion(f32[2,128,512]{2,1,0:T(8,128)S(1)} %get-tuple-element.990, bf16[4,2,128,648]{3,2,1,0:T(8,128)(2,1)S(1)} %get-tuple-element.1010, s32[]{:T(128)S(6)} %select_n.326, s32[]{:T(128)S(6)} %select_n.328, f32[]{:T(128)} %bitcast.184, s32[]{:T(128)S(6)} %select_n.330, f32[]{:T(128)} %bitcast.187, ...), kind=kLoop, calls=%fused_computation.11.clone.1 | loop fusion | flops 1703936 | bytes 2097189 | tf_op jit(solution)/shard_map/while/body/eval_jaxpr/while/body/eval_jaxpr/add | solution.py:88
  227.8 0.6 dynamic_slice.276
  231.0 0.7 constant_dynamic-slice_fusion.14
  231.6 3.1 %bitcast_add_fusion.14 = f32[2,128,512]{2,1,0:T(8,128)S(1)} fusion(f32[2,128,512]{2,1,0:T(8,128)S(1)} %get-tuple-element.990, bf16[4,2,128,648]{3,2,1,0:T(8,128)(2,1)S(1)} %get-tuple-element.1010, s32[]{:T(128)S(6)} %select_n.326, s32[]{:T(128)S(6)} %select_n.328, f32[]{:T(128)} %bitcast.184, s32[]{:T(128)S(6)} %select_n.330, f32[]{:T(128)} %bitcast.187, ...), kind=kLoop, calls=%fused_computation.11.clone.1 | loop fusion | flops 1703936 | bytes 2097189 | tf_op jit(solution)/shard_map/while/body/eval_jaxpr/while/body/eval_jaxpr/add | solution.py:88
  234.8 0.6 dynamic_slice.276
  238.0 0.7 constant_dynamic-slice_fusion.14
  238.7 3.1 %bitcast_add_fusion.14 = f32[2,128,512]{2,1,0:T(8,128)S(1)} fusion(f32[2,128,512]{2,1,0:T(8,128)S(1)} %get-tuple-element.990, bf16[4,2,128,648]{3,2,1,0:T(8,128)(2,1)S(1)} %get-tuple-element.1010, s32[]{:T(128)S(6)} %select_n.326, s32[]{:T(128)S(6)} %select_n.328, f32[]{:T(128)} %bitcast.184, s32[]{:T(128)S(6)} %select_n.330, f32[]{:T(128)} %bitcast.187, ...), kind=kLoop, calls=%fused_computation.11.clone.1 | loop fusion | flops 1703936 | bytes 2097189 | tf_op jit(solution)/shard_map/while/body/eval_jaxpr/while/body/eval_jaxpr/add | solution.py:88
  241.9 0.8 copy-done
  (47 shorter events, 8.1 us)
Async XLA Ops:
  6.5 32.2 %copy-start.3 = (f32[4,4,4]{2,1,0:T(4,128)S(1)}, f32[4,4,4]{2,1,0:T(4,128)}, u32[]{:S(2)}) copy-start(f32[4,4,4]{2,1,0:T(4,128)} %param.15) | copy-start | bytes 772
  6.5 32.2 %copy-start.4 = (s32[4,4]{1,0:T(4,128)S(1)}, s32[4,4]{1,0:T(4,128)}, u32[]{:S(2)}) copy-start(s32[4,4]{1,0:T(4,128)} %param.16) | copy-start | bytes 196
  6.5 30.4 %all-gather.3.cloned.1.call-start = ((), (), s32[]{:S(2)}) async-start(), calls=%async_computation | async-start | bytes 1310720 | tf_op jit(solution)/shard_map/all_gather | solution.py:109
  7.3 204.6 %all-gather.5.cloned.1.call-start = ((), (), s32[]{:S(2)}) async-start(), calls=%async_computation.1 | async-start | bytes 1310720 | tf_op jit(solution)/shard_map/all_gather | solution.py:162
  38.8 41.0 %copy-start.2 = (bf16[2,256,256]{2,1,0:T(8,128)(2,1)S(1)}, bf16[2,256,256]{2,1,0:T(8,128)(2,1)}, u32[]{:S(2)}) copy-start(bf16[2,256,256]{2,1,0:T(8,128)(2,1)} %param.17) | copy-start | bytes 786436
  74.1 10.5 %collective-permute-start = (f32[1,2,128,512]{3,2,1,0:T(8,128)S(1)}, f32[1,2,128,512]{3,2,1,0:T(8,128)S(1)}, u32[]{:S(2)}, u32[]{:S(2)}) collective-permute-start(f32[1,2,128,512]{3,2,1,0:T(8,128)S(1)} %bitcast.195), channel_id=1, source_target_pairs={{0,1},{1,2},{2,3},{3,4},{4,5},{5,6},{6,7},{8,9},{9,10},{10,11},{11... | collective-permute-start | bytes 1572872 | tf_op jit(solution)/shard_map/ppermute | solution.py:16
  76.1 10.3 %collective-permute-start.1 = (f32[1,2,128,512]{3,2,1,0:T(8,128)S(1)}, f32[1,2,128,512]{3,2,1,0:T(8,128)S(1)}, u32[]{:S(2)}, u32[]{:S(2)}) collective-permute-start(f32[1,2,128,512]{3,2,1,0:T(8,128)S(1)} %bitcast.196), channel_id=1, source_target_pairs={{1,0},{2,1},{3,2},{4,3},{5,4},{6,5},{7,6},{9,8},{10,9},{11,10},{12... | collective-permute-start | bytes 1572872 | tf_op jit(solution)/shard_map/ppermute | solution.py:19
  100.5 3.2 %copy-start.1 = (bf16[1,4,256,256]{3,2,1,0:T(8,128)(2,1)S(1)}, bf16[1,4,256,256]{3,2,1,0:T(8,128)(2,1)}, u32[]{:S(2)}) copy-start(bf16[1,4,256,256]{3,2,1,0:T(8,128)(2,1)} %param.21) | copy-start | bytes 1572868
  112.1 1.8 copy-start.5
  112.1 1.8 copy-start.6
  169.8 7.7 %collective-permute-start.2 = (bf16[1,2,128,512]{3,2,1,0:T(8,128)(2,1)S(1)}, bf16[1,2,128,512]{3,2,1,0:T(8,128)(2,1)S(1)}, u32[]{:S(2)}, u32[]{:S(2)}) collective-permute-start(bf16[1,2,128,512]{3,2,1,0:T(8,128)(2,1)S(1)} %get-tuple-element.721), channel_id=1, source_target_pairs={{0,1},{1,2},{2,3},{3,4},{4,5},{5,6},{6,7},{8,9},{9,10},{10,11},{11... | collective-permute-start | bytes 786440 | tf_op jit(solution)/shard_map/ppermute | solution.py:27
  175.4 6.2 %collective-permute-start.3 = (bf16[1,2,128,512]{3,2,1,0:T(8,128)(2,1)S(1)}, bf16[1,2,128,512]{3,2,1,0:T(8,128)(2,1)S(1)}, u32[]{:S(2)}, u32[]{:S(2)}) collective-permute-start(bf16[1,2,128,512]{3,2,1,0:T(8,128)(2,1)S(1)} %get-tuple-element.722), channel_id=1, source_target_pairs={{1,0},{2,1},{3,2},{4,3},{5,4},{6,5},{7,6},{9,8},{10,9},{11,10},{12... | collective-permute-start | bytes 786440 | tf_op jit(solution)/shard_map/ppermute | solution.py:27
  241.9 0.8 copy-start
Sparse Core Ops, SparseCore 0:
  9.2 27.6 all-gather.2
  182.6 29.1 all-gather.4
where the time goes:
time: 252 us; the launch traced here: 249 us
  waiting for transfers between devices  66.2 us (26%)
  local copies, waits for them, and re-layouts  62 us (25%)
  loops' own time  44.3 us (18%)
  other arithmetic  43.1 us (17%)
  between operations  14.3 us (6%)
  starting transfers between devices  13.2 us (5%)
  matrix products  6.44 us (3%)
    dynamic_update_slice x4, local copies, waits for them, and re-layouts, place(): lax.dynamic_update_slice(acc, current + gradients[which][None], corner)  30.3 us
    all_gather x1, waiting for transfers between devices, per_device(): fold_piece = lax.all_gather(image, 'ang', axis=0, tiled=True)  29.4 us
    all_gather x1, waiting for transfers between devices, per_device(): piece = lax.all_gather(slab, 'ang', axis=0, tiled=True)  25.3 us
    add x8, other arithmetic, add_taps(): total = total + shear_taps[tap, angle, depth] * piece.astype(jnp.float32)  24.8 us
    another operation x1, loops' own time, one_angle(): current = lax.fori_loop(0, piece.shape[0], add_slice, acc[which])  18 us
    another operation x1, loops' own time, per_device(): lax.fori_loop(0, count_all, place, jnp.zeros(extended.shape, jnp.float32))  15.7 us
    gather x12, local copies, waits for them, and re-layouts  12.1 us
    another operation x1, loops' own time, one_slice(): current = lax.fori_loop(0, fold_piece.shape[0], add_angle, acc[which])  10.6 us
  transfers between devices with their start and end apart: 6, of which 6 were waited for; matrix products, arithmetic and copies ran while one was open for 1% of the time, Pallas kernels for 0%

commit v1 on v0

v1 whole, which is shorter than its diff:
```python
import functools
import math

import jax
import jax.numpy as jnp
import ml_dtypes
import numpy as np
from jax import lax
from jax.experimental import pallas as pl
from jax.experimental.pallas import tpu as pltpu
from jax.sharding import PartitionSpec as P

MESH = pl.DeviceIdType.MESH
BF = jnp.bfloat16
F32 = jnp.float32


def dft_blocks(length):
    index = np.arange(length)
    phase = (np.outer(index, index) % length).astype(np.float32) * np.float32(2.0 * math.pi / length)
    scale = np.float32(1.0 / math.sqrt(length))
    cosine = (np.cos(phase) * scale).astype(ml_dtypes.bfloat16)
    sine = (np.sin(phase) * scale).astype(ml_dtypes.bfloat16)
    first = np.block([[cosine, sine], [-sine, cosine]])
    return first, np.ascontiguousarray(first.T)


def kernel(
    n, strips, chunks, slab, taps, offsets, probe, scan_rows, scan_columns, counts, amplitudes,
    wf, wg, out, ga, gb, bands_f, bands_b, ext, acc, edges, edge_in, img,
    a_send, a_recv, h_send, h_recv, e_send, e_recv, b_send, b_recv,
):
    rows, width = slab.shape[2], slab.shape[3]
    length = probe.shape[1]
    slots = amplitudes.shape[1]
    tap_count = taps.shape[0]
    size = rows // chunks
    ang = lax.axis_index("ang")
    strip = lax.axis_index("strip")
    has_up = strip > 0
    has_down = strip < strips - 1
    square = n == 4
    if square:
        ax, ay = ang % 2, ang // 2
        near_x, near_y = ay * 2 + (1 - ax), (1 - ay) * 2 + ax
        order = [ang, near_x, near_y, (1 - ay) * 2 + (1 - ax)]
        peers = [near_x, near_y]
    else:
        order = [(ang + n - k) % n for k in range(n)]
        peers = [(ang + k) % n for k in range(1, n)]

    barrier = pltpu.get_barrier_semaphore()
    for peer in peers:
        pl.semaphore_signal(barrier, inc=1, device_id=(peer, strip), device_id_type=MESH)

    @pl.when(has_up)
    def _():
        pl.semaphore_signal(barrier, inc=1, device_id=(ang, strip - 1), device_id_type=MESH)

    @pl.when(has_down)
    def _():
        pl.semaphore_signal(barrier, inc=1, device_id=(ang, strip + 1), device_id_type=MESH)

    sides = (strip + strips - 1) // strips + 1 - (strip + 1) // strips
    pl.semaphore_wait(barrier, len(peers) + sides)

    def part(c):
        return pl.ds(c * size, size)

    def copy(src, dst, send, recv, device):
        return pltpu.make_async_remote_copy(
            src_ref=src, dst_ref=dst, send_sem=send, recv_sem=recv,
            device_id=device, device_id_type=MESH,
        )

    def gather_copy(own, g, send, recv, c, kind):
        if square and kind == 2:
            source, peer = (1, near_y) if c % 2 == 0 else (2, near_x)
            source = g.at[source, :, part(c), :]
        else:
            source, peer = own.at[:, part(c), :], peers[kind]
        return copy(
            source, g.at[kind + 1, :, part(c), :], send.at[kind, c], recv.at[kind, c], (peer, strip)
        )

    def gather_start(own, g, send, recv, c):
        for kind in range(len(peers)):
            gather_copy(own, g, send, recv, c, kind).start()

    def gather_forward(own, g, send, recv, c):
        if square:
            gather_copy(own, g, send, recv, c, c % 2).wait_recv()
            gather_copy(own, g, send, recv, c, 2).start()

    def gather_wait(own, g, send, recv, c):
        for kind in range(n - 1):
            if not (square and kind == c % 2):
                gather_copy(own, g, send, recv, c, kind).wait_recv()

    def gather_sent(own, g, send, recv):
        for c in range(chunks):
            for kind in range(n - 1):
                gather_copy(own, g, send, recv, c, kind).wait_send()

    def strip_copy(src, dst, send, recv, c, way):
        return copy(
            src.at[:, part(c), :], dst.at[way, :, part(c), :], send.at[way, c], recv.at[way, c],
            (ang, strip - 1 if way == 0 else strip + 1),
        )

    def halo_copy(c, way):
        target = 2 * rows if way == 0 else 0
        return copy(
            ext.at[:, pl.ds(rows + c * size, size), :],
            ext.at[:, pl.ds(target + c * size, size), :],
            h_send.at[way, c], h_recv.at[way, c], (ang, strip - 1 if way == 0 else strip + 1),
        )

    def band(k, sign, store):
        if sign > 0:
            angle, depth = ang, order[k]
        else:
            angle, depth = order[k], ang
        offset = offsets[angle, depth]
        weights = [taps[t, angle, depth] for t in range(tap_count)]
        step = 64

        @pl.loop(0, width // step)
        def _(i):
            shape = (step, width)
            source = lax.broadcasted_iota(jnp.int32, shape, 0) + i * step
            target = lax.broadcasted_iota(jnp.int32, shape, 1)
            tap = (source - target) * sign - offset
            value = jnp.zeros(shape, F32)
            for t in range(tap_count):
                value = jnp.where(tap == t, weights[t], value)
            store[k, pl.ds(pl.multiple_of(i * step, step), step), :] = value.astype(BF)

    def apply(own, g, bands, c):
        total = None
        for k in range(n):
            block = own[:, part(c), :] if k == 0 else g[k, :, part(c), :]
            term = jnp.dot(
                block.reshape(2 * size, width), bands[k], preferred_element_type=F32
            )
            total = term if total is None else total + term
        return total.reshape(2, size, width)

    first = slab.at[0]
    for c in range(chunks):
        gather_start(first, ga, a_send, a_recv, c)
    for k in range(n):
        band(k, 1, bands_f)
    for c in range(chunks):
        gather_forward(first, ga, a_send, a_recv, c)
    for k in range(n):
        band(k, -1, bands_b)
    acc[...] = jnp.zeros_like(acc)
    for c in range(chunks):
        gather_wait(first, ga, a_send, a_recv, c)
        piece = apply(first, ga, bands_f, c)
        ext[:, pl.ds(rows + c * size, size), :] = piece.astype(BF)

        @pl.when(has_up)
        def _():
            halo_copy(c, 0).start()

        @pl.when(has_down)
        def _():
            halo_copy(c, 1).start()

    @pl.when(has_up)
    def _():
        for c in range(chunks):
            halo_copy(c, 1).wait_recv()

    @pl.when(jnp.logical_not(has_up))
    def _():
        ext[:, :rows, :] = jnp.zeros((2, rows, width), BF)

    @pl.when(has_down)
    def _():
        for c in range(chunks):
            halo_copy(c, 0).wait_recv()

    @pl.when(jnp.logical_not(has_down))
    def _():
        ext[:, 2 * rows :, :] = jnp.zeros((2, rows, width), BF)

    def picks(shape, first, second, shift, live=None):
        hit = (
            lax.broadcasted_iota(jnp.int32, shape, second)
            - lax.broadcasted_iota(jnp.int32, shape, first)
        ) == shift
        if live is not None:
            hit = jnp.logical_and(hit, live)
        return jnp.where(hit, 1.0, 0.0).astype(BF)

    tall = length + rows

    def frame(f, carry):
        row = scan_rows[0, f]
        column = scan_columns[0, f]
        probe_real = probe[0].astype(F32)
        probe_imag = probe[1].astype(F32)
        cut = jnp.dot(
            ext[...].reshape(2 * tall, width), picks((width, length), 1, 0, column),
            preferred_element_type=F32,
        ).astype(BF)
        patch = jnp.dot(
            picks((length, tall), 0, 1, row),
            jnp.concatenate([cut[:tall], cut[tall:]], axis=1),
            preferred_element_type=F32,
        )
        patch_real, patch_imag = patch[:, :length], patch[:, length:]
        wave = jnp.concatenate(
            [
                (probe_real * patch_real - probe_imag * patch_imag).astype(BF),
                (probe_real * patch_imag + probe_imag * patch_real).astype(BF),
            ],
            axis=0,
        )
        half = jnp.dot(wf[...], wave, preferred_element_type=F32).astype(BF)
        half = jnp.concatenate([half[:length], half[length:]], axis=1)
        far = jnp.dot(half, wg[...], preferred_element_type=F32)
        far_real, far_imag = far[:, :length], far[:, length:]
        factor = 1.0 - amplitudes[0, f].astype(F32) * lax.rsqrt(
            far_real * far_real + far_imag * far_imag + 1.0
        )
        residual = jnp.concatenate(
            [(far_real * factor).astype(BF), (far_imag * factor).astype(BF)], axis=0
        )
        back_half = jnp.dot(wg[...], residual, preferred_element_type=F32).astype(BF)
        back_half = jnp.concatenate([back_half[:length], back_half[length:]], axis=1)
        back = jnp.dot(back_half, wf[...], preferred_element_type=F32)
        back_real, back_imag = back[:, :length], back[:, length:]
        grad = jnp.concatenate(
            [
                (probe_real * back_real + probe_imag * back_imag).astype(BF),
                (probe_real * back_imag - probe_imag * back_real).astype(BF),
            ],
            axis=0,
        )
        placed = jnp.dot(
            grad, picks((length, width), 0, 1, column), preferred_element_type=F32
        ).astype(BF)
        shape = (tall, length)
        live = lax.broadcasted_iota(jnp.int32, shape, 0) * 0 + f < counts[0, 0]
        placed = jnp.dot(
            picks(shape, 1, 0, row, live),
            jnp.concatenate([placed[:length], placed[length:]], axis=1),
            preferred_element_type=F32,
        )
        acc[0] += placed[:, :width]
        acc[1] += placed[:, width:]
        return carry

    lax.fori_loop(0, slots, frame, 0)

    for c in range(chunks):
        for way, base in ((0, 0), (1, 2 * rows)):
            edges[way, :, part(c), :] = acc[:, pl.ds(base + c * size, size), :].astype(BF)

        @pl.when(has_up)
        def _():
            strip_copy(edges.at[0], edge_in, e_send, e_recv, c, 0).start()

        @pl.when(has_down)
        def _():
            strip_copy(edges.at[1], edge_in, e_send, e_recv, c, 1).start()

    for c in range(chunks):
        middle = pl.ds(rows + c * size, size)

        @pl.when(has_up)
        def _():
            strip_copy(edges.at[1], edge_in, e_send, e_recv, c, 1).wait_recv()
            acc[:, middle, :] += edge_in[1, :, part(c), :].astype(F32)

        @pl.when(has_down)
        def _():
            strip_copy(edges.at[0], edge_in, e_send, e_recv, c, 0).wait_recv()
            acc[:, middle, :] += edge_in[0, :, part(c), :].astype(F32)

        img[:, part(c), :] = acc[:, middle, :].astype(BF)
        gather_start(img, gb, b_send, b_recv, c)
    for c in range(chunks):
        gather_forward(img, gb, b_send, b_recv, c)
    for c in range(chunks):
        gather_wait(img, gb, b_send, b_recv, c)
        out[0, :, part(c), :] = apply(img, gb, bands_b, c)

    gather_sent(first, ga, a_send, a_recv)
    gather_sent(img, gb, b_send, b_recv)
    for way, here in ((0, has_up), (1, has_down)):

        @pl.when(here)
        def _(way=way):
            for c in range(chunks):
                halo_copy(c, way).wait_send()
                strip_copy(edges.at[way], edge_in, e_send, e_recv, c, way).wait_send()


def per_device(
    n, strips, slab, shear_taps, band_offsets, probe, scan_rows, scan_columns, frame_counts, amplitudes
):
    rows, width = slab.shape[2], slab.shape[3]
    length = probe.shape[1]
    chunks = 2
    wf, wg = dft_blocks(length)
    vmem = pl.BlockSpec(memory_space=pltpu.VMEM)
    smem = pl.BlockSpec(memory_space=pltpu.SMEM)
    dma = pltpu.SemaphoreType.DMA
    field = (2, rows, width)
    return pl.pallas_call(
        functools.partial(kernel, n, strips, chunks),
        out_shape=jax.ShapeDtypeStruct((1,) + field, F32),
        in_specs=[vmem, smem, smem, vmem, smem, smem, smem, vmem, vmem, vmem],
        out_specs=vmem,
        scratch_shapes=[
            pltpu.VMEM((n,) + field, BF),
            pltpu.VMEM((n,) + field, BF),
            pltpu.VMEM((n, width, width), BF),
            pltpu.VMEM((n, width, width), BF),
            pltpu.VMEM((2, length + rows, width), BF),
            pltpu.VMEM((2, length + rows, width), F32),
            pltpu.VMEM((2,) + field, BF),
            pltpu.VMEM((2,) + field, BF),
            pltpu.VMEM(field, BF),
            dma((n - 1, chunks)), dma((n - 1, chunks)),
            dma((2, chunks)), dma((2, chunks)),
            dma((2, chunks)), dma((2, chunks)),
            dma((n - 1, chunks)), dma((n - 1, chunks)),
        ],
        compiler_params=pltpu.CompilerParams(
            collective_id=0, has_side_effects=True, vmem_limit_bytes=48 << 20
        ),
    )(
        slab, shear_taps, band_offsets, probe, scan_rows, scan_columns, frame_counts, amplitudes,
        jnp.asarray(wf), jnp.asarray(wg),
    )


def solution(mesh):
    return jax.shard_map(
        functools.partial(per_device, mesh.shape["ang"], mesh.shape["strip"]),
        mesh=mesh,
        in_specs=(
            P("ang", None, "strip", None),
            P(),
            P(),
            P(),
            P("ang", "strip"),
            P("ang", "strip"),
            P("ang", "strip"),
            P("ang", "strip", None, None),
        ),
        out_specs=P("ang", None, "strip", None),
        check_vma=False,
    )
```

time: 252 us -> 54.1 us (0.21)
  waiting for transfers between devices: 66.2 us -> 0 us
  local copies, waits for them, and re-layouts: 62 us -> 7.2 us
  Pallas kernels: 0 us -> 45.8 us
  loops' own time: 44.3 us -> 0 us
  other arithmetic: 43.1 us -> 0 us
  between operations: 14.3 us -> 0.72 us
  starting transfers between devices: 13.2 us -> 0 us
  matrix products: 6.44 us -> 0 us
    all_gather x2 -> x0, waiting for transfers between devices: 54.7 us -> none  [the longest x1 29.4 us: per_device(): fold_piece = lax.all_gather(image, 'ang', axis=0, tiled=True)]
    pallas_call x0 -> x1, Pallas kernels: none -> 45.8 us  [per_device(): pl.pallas_call(functools.partial(kernel, n, strips, chunks), out_shape=ja...]
    another operation x4 -> x0, loops' own time: 44.3 us -> none  [the longest x1 18 us: one_angle(): current = lax.fori_loop(0, piece.shape[0], add_slice, acc[which])]
    dynamic_update_slice x4 -> x0, local copies, waits for them, and re-layouts: 30.3 us -> none  [place(): lax.dynamic_update_slice(acc, current + gradients[which][None], corner)]
    add x12 -> x0, other arithmetic: 29.9 us -> none  [the longest x8 24.8 us: add_taps(): total = total + shear_taps[tap, angle, depth] * piece.astype(jnp.float32)]
    dynamic_slice x24 -> x0, local copies, waits for them, and re-layouts: 14.9 us -> none  [the longest x8 5.44 us: add_taps(): total = total + shear_taps[tap, angle, depth] * piece.astype(jnp.float32)]
    ppermute x4 -> x0, starting transfers between devices: 13.1 us -> none  [the longest x2 7.56 us: shifted(): return lax.ppermute(block, axis, route)]
    gather x12 -> x0, local copies, waits for them, and re-layouts: 12.1 us -> none
  transfers between devices with their start and end apart: 6 -> 0, of which waited for: 6 -> 0; matrix products, arithmetic and copies ran while one was open for 1% -> 0% of each run, Pallas kernels for 0% -> 0%
where the time goes in v1:
time: 54.1 us; the launch traced here: 53.7 us
  Pallas kernels  45.8 us (85%)
  local copies, waits for them, and re-layouts  7.2 us (13%)
  between operations  0.72 us (1%)
    pallas_call x1, Pallas kernels, per_device(): pl.pallas_call(functools.partial(kernel, n, strips, chunks), out_shape=ja...  45.8 us
    unnamed x19, local copies, waits for them, and re-layouts  7.2 us

profile of v1, /device:TPU:16, one launch (start us, length us, event | category | flops | bytes accessed | tf_op | source)
XLA Modules:
  0.0 53.7 jit_solution(673262864664456477)
XLA Ops:
  0.0 0.0 copy-start.8
  0.0 0.0 copy-start.7
  0.7 0.0 copy-done.8
  0.7 0.0 copy-done.7
  0.7 0.0 copy-start
  0.7 1.0 %copy-done = bf16[1,4,256,256]{3,2,1,0:T(8,128)(2,1)S(1)} copy-done((bf16[1,4,256,256]{3,2,1,0:T(8,128)(2,1)S(1)}, bf16[1,4,256,256]{3,2,1,0:T(8,128)(2,1)}, u32[]{:S(2)}) %copy-start) | copy-done | bytes 524312
  1.7 0.0 copy-start.1
  1.7 1.0 %copy-done.1 = bf16[512,512]{1,0:T(8,128)(2,1)S(1)} copy-done((bf16[512,512]{1,0:T(8,128)(2,1)S(1)}, bf16[512,512]{1,0:T(8,128)(2,1)}, u32[]{:S(2)}) %copy-start.1) | copy-done | bytes 524312
  2.8 0.0 copy-start.2
  2.8 1.0 %copy-done.2 = bf16[512,512]{1,0:T(8,128)(2,1)S(1)} copy-done((bf16[512,512]{1,0:T(8,128)(2,1)S(1)}, bf16[512,512]{1,0:T(8,128)(2,1)}, u32[]{:S(2)}) %copy-start.2) | copy-done | bytes 524312
  3.8 0.0 copy-start.3
  3.8 0.9 %copy-done.3 = bf16[1,2,128,512]{3,2,1,0:T(8,128)(2,1)S(1)} copy-done((bf16[1,2,128,512]{3,2,1,0:T(8,128)(2,1)S(1)}, bf16[1,2,128,512]{3,2,1,0:T(8,128)(2,1)}, u32[]{:S(2)}) %copy-start.3) | copy-done | bytes 262168
  4.8 0.0 copy-start.4
  4.8 0.9 %copy-done.4 = bf16[2,256,256]{2,1,0:T(8,128)(2,1)S(1)} copy-done((bf16[2,256,256]{2,1,0:T(8,128)(2,1)S(1)}, bf16[2,256,256]{2,1,0:T(8,128)(2,1)}, u32[]{:S(2)}) %copy-start.4) | copy-done | bytes 262168
  5.7 0.0 copy-start.5
  5.7 0.7 %copy-done.5 = f32[4,4,4]{2,1,0:T(4,128)S(1)} copy-done((f32[4,4,4]{2,1,0:T(4,128)S(1)}, f32[4,4,4]{2,1,0:T(4,128)}, u32[]{:S(2)}) %copy-start.5) | copy-done | bytes 280
  6.4 0.0 copy-start.6
  6.4 0.7 %copy-done.6 = s32[4,4]{1,0:T(4,128)S(1)} copy-done((s32[4,4]{1,0:T(4,128)S(1)}, s32[4,4]{1,0:T(4,128)}, u32[]{:S(2)}) %copy-start.6) | copy-done | bytes 88
  7.1 45.8 %shard_map.100 = f32[1,2,128,512]{3,2,1,0:T(8,128)S(1)} custom-call(bf16[1,2,128,512]{3,2,1,0:T(8,128)(2,1)S(1)} %copy-done.3, f32[4,4,4]{2,1,0:T(4,128)S(1)} %copy-done.5, s32[4,4]{1,0:T(4,128)S(1)} %copy-done.6, bf16[2,256,256]{2,1,0:T(8,128)(2,1)S(1)} %copy-done.4, s32[1,4]{1,0:T(1,128)S(1)} %copy-done.7, s32[1,4]{1,0:T(1,128)S(1)} %copy-done.8, ...), custom_call_target="tpu_custom_call" | custom-call | tf_op jit(solution)/shard_map/pallas_call | solution.py:315
  52.9 0.8 %copy.13 = f32[1,2,128,512]{3,2,1,0:T(8,128)} copy(f32[1,2,128,512]{3,2,1,0:T(8,128)S(1)} %shard_map.100) | data formatting | bytes 1048576
Async XLA Ops:
  0.0 0.7 %copy-start.8 = (s32[1,4]{1,0:T(1,128)S(1)}, s32[1,4]{1,0:T(1,128)}, u32[]{:S(2)}) copy-start(s32[1,4]{1,0:T(1,128)} %scan_columns.1) | copy-start | bytes 52
  0.0 0.7 %copy-start.7 = (s32[1,4]{1,0:T(1,128)S(1)}, s32[1,4]{1,0:T(1,128)}, u32[]{:S(2)}) copy-start(s32[1,4]{1,0:T(1,128)} %scan_rows.1) | copy-start | bytes 52
  0.7 1.0 %copy-start = (bf16[1,4,256,256]{3,2,1,0:T(8,128)(2,1)S(1)}, bf16[1,4,256,256]{3,2,1,0:T(8,128)(2,1)}, u32[]{:S(2)}) copy-start(bf16[1,4,256,256]{3,2,1,0:T(8,128)(2,1)} %amplitudes.1) | copy-start | bytes 1572868
  1.7 1.0 %copy-start.1 = (bf16[512,512]{1,0:T(8,128)(2,1)S(1)}, bf16[512,512]{1,0:T(8,128)(2,1)}, u32[]{:S(2)}) copy-start(bf16[512,512]{1,0:T(8,128)(2,1)} %constant.5.clone.wg) | copy-start | bytes 1572868
  2.8 1.0 %copy-start.2 = (bf16[512,512]{1,0:T(8,128)(2,1)S(1)}, bf16[512,512]{1,0:T(8,128)(2,1)}, u32[]{:S(2)}) copy-start(bf16[512,512]{1,0:T(8,128)(2,1)} %constant.4.clone.wf) | copy-start | bytes 1572868
  3.8 0.9 %copy-start.3 = (bf16[1,2,128,512]{3,2,1,0:T(8,128)(2,1)S(1)}, bf16[1,2,128,512]{3,2,1,0:T(8,128)(2,1)}, u32[]{:S(2)}) copy-start(bf16[1,2,128,512]{3,2,1,0:T(8,128)(2,1)} %slab.1) | copy-start | bytes 786436
  4.8 0.9 %copy-start.4 = (bf16[2,256,256]{2,1,0:T(8,128)(2,1)S(1)}, bf16[2,256,256]{2,1,0:T(8,128)(2,1)}, u32[]{:S(2)}) copy-start(bf16[2,256,256]{2,1,0:T(8,128)(2,1)} %probe.1) | copy-start | bytes 786436
  5.7 0.7 %copy-start.5 = (f32[4,4,4]{2,1,0:T(4,128)S(1)}, f32[4,4,4]{2,1,0:T(4,128)}, u32[]{:S(2)}) copy-start(f32[4,4,4]{2,1,0:T(4,128)} %taps.1) | copy-start | bytes 772
  6.4 0.7 %copy-start.6 = (s32[4,4]{1,0:T(4,128)S(1)}, s32[4,4]{1,0:T(4,128)}, u32[]{:S(2)}) copy-start(s32[4,4]{1,0:T(4,128)} %offsets.1) | copy-start | bytes 196
